TPU v7x, 256 devices: a whole 4x4x8 slice. The times are simulated.
256 devices in a mesh: pb: 16 (over x, y), aux: 16 (over z, core).
Axes of the slice: x: 4, y: 4, z: 8, core: 2. Of those that a mesh axis runs over, the one named last changes fastest.
Arguments:
- ao_blocks: float32 [16, 4, 640, 2, 6400], P('pb', None, 'aux'), may hold values from -1 to 1
- occ_coef: float32 [27, 2, 80, 16], replicated, may hold values from -0.625 to 0.625
- vir_coef: float32 [27, 2, 80, 64], replicated, may hold values from -0.625 to 0.625
- occ_energy: float32 [27, 16], replicated, may hold values from -2.5 to -0.5
- vir_energy: float32 [27, 64], replicated, may hold values from 0.5 to 4
- kpoint_diff: int32 [27, 27], replicated, may hold values from 0 to 26, as said below
- transfer_label: int32 [16], replicated, may hold values from 1 to 26, as said below
- chosen_rows: int32 [16, 4], replicated, may hold values from 0 to 26, as said below
Outputs:
- amplitudes: float32 [16, 2, 2, 2, 16, 16, 4096], P('pb', None, None, None, 'aux')
Inputs may be any that keep to these rules, and one draw needn't show every extreme that they name: The k-points are the points of a 3 x 3 x 3 periodic mesh under a relabeling drawn from the seed, with label 0 for the zero transfer; kpoint_diff[k, q] is the label of k - q modulo the mesh, so it is a group table. `transfer_label`: the labels are nonzero transfers, all different; slots 2m and 2m + 1 hold opposite transfers, q and -q. `chosen_rows`: the four entries of each row are different k labels.
All inputs are finite; a program needn't handle non-finite values.
Results may differ from a plain program's by a relative error of at most 0.0001.
Values sent between devices are 32-bit elements; how exact they have to be, the bound alone decides.
A program may use at most 128 MiB of HBM per device.

v0:
```python
import jax
import jax.numpy as jnp
from jax import lax
from jax.sharding import PartitionSpec as P


def partner_2(value, axis, distance):
    mask = 2**distance
    pairs = [(source, source ^ mask) for source in range(lax.axis_size(axis))]
    return lax.ppermute(value, axis, pairs)


def to_orbitals(blocks, occ_sel, vir_sel):
    highest = lax.Precision.HIGHEST
    ao_width = occ_sel.shape[2]
    complex_ao = blocks.reshape(blocks.shape[0], blocks.shape[1], 2, ao_width, ao_width)
    real_ao = complex_ao[:, :, 0]
    imag_ao = complex_ao[:, :, 1]
    occ_real = occ_sel[:, 0]
    occ_imag = occ_sel[:, 1]
    half_real = jnp.einsum("smi,spmn->spin", occ_real, real_ao, precision=highest) + jnp.einsum(
        "smi,spmn->spin", occ_imag, imag_ao, precision=highest
    )
    half_imag = jnp.einsum("smi,spmn->spin", occ_real, imag_ao, precision=highest) - jnp.einsum(
        "smi,spmn->spin", occ_imag, real_ao, precision=highest
    )
    vir_real = vir_sel[:, 0]
    vir_imag = vir_sel[:, 1]
    full_real = jnp.einsum("spin,sna->spia", half_real, vir_real, precision=highest) - jnp.einsum(
        "spin,sna->spia", half_imag, vir_imag, precision=highest
    )
    full_imag = jnp.einsum("spin,sna->spia", half_real, vir_imag, precision=highest) + jnp.einsum(
        "spin,sna->spia", half_imag, vir_real, precision=highest
    )
    return jnp.concatenate([full_real, full_imag], axis=3)


def pair_sums(left_side, right_side, vir_width):
    highest = lax.Precision.HIGHEST
    pattern = "spia,tpjb->stijab"
    left_real = left_side[..., :vir_width]
    left_imag = left_side[..., vir_width:]
    right_real = right_side[..., :vir_width]
    right_imag = right_side[..., vir_width:]
    real_part = jnp.einsum(pattern, left_real, right_real, precision=highest) - jnp.einsum(
        pattern, left_imag, right_imag, precision=highest
    )
    imag_part = jnp.einsum(pattern, left_real, right_imag, precision=highest) + jnp.einsum(
        pattern, left_imag, right_real, precision=highest
    )
    return (real_part, imag_part)


def make_amplitudes(real_part, imag_part, occ_left, occ_right, vir_left, vir_right):
    denominator = (
        occ_left[:, None, :, None, None, None]
        + occ_right[None, :, None, :, None, None]
        - vir_left[:, None, None, None, :, None]
        - vir_right[None, :, None, None, None, :]
    )
    result = jnp.stack([real_part / denominator, imag_part / denominator])
    shape_now = result.shape
    return result.reshape(
        shape_now[0],
        shape_now[1],
        shape_now[2],
        shape_now[3],
        shape_now[4],
        shape_now[5] * shape_now[6],
    )


def per_device(
    ao_blocks, occ_coef, vir_coef, occ_energy, vir_energy, kpoint_diff, transfer_label, chosen_rows
):
    vir_width = vir_coef.shape[3]
    own_slot = lax.axis_index("pb")
    partner = jnp.bitwise_xor(own_slot, 1)
    own_rows = chosen_rows[own_slot]
    own_vir = kpoint_diff[own_rows, transfer_label[own_slot]]
    other_rows = chosen_rows[partner]
    other_vir = kpoint_diff[other_rows, transfer_label[partner]]
    own_orbitals = to_orbitals(ao_blocks[0], occ_coef[own_rows], vir_coef[own_vir])
    ia_side = lax.all_to_all(own_orbitals[0:2], "aux", split_axis=2, concat_axis=1, tiled=True)
    rows_here = ia_side.shape[2]
    row_start = lax.axis_index("aux") * rows_here
    occ_left = lax.dynamic_slice_in_dim(occ_energy[own_rows[0:2]], row_start, rows_here, 1)
    occ_right = occ_energy[other_rows[2:4]]
    vir_left = vir_energy[own_vir[0:2]]
    vir_right = vir_energy[other_vir[2:4]]
    jb_side = own_orbitals[2:4]
    gathered = lax.all_gather(jb_side, "aux", axis=1, tiled=True)
    partner_side = partner_2(gathered, "pb", 0)
    real_part, imag_part = pair_sums(ia_side, partner_side, vir_width)
    result = make_amplitudes(real_part, imag_part, occ_left, occ_right, vir_left, vir_right)
    return result[None]


def solution(mesh):
    in_specs = (P("pb", None, "aux", None, None), P(), P(), P(), P(), P(), P(), P())
    out_specs = P("pb", None, None, None, "aux", None, None)
    return jax.shard_map(
        per_device, mesh=mesh, in_specs=in_specs, out_specs=out_specs, check_vma=False
    )
```

profile of v0, /device:TPU:1, one launch (start us, length us, event | category | flops | bytes accessed | tf_op | source)
XLA Modules:
  0.0 467.7 jit_solution(12842340600891097625)
XLA Ops:
  6.5 1.4 fusion.29
  9.3 1.0 fusion.27
  10.9 7.1 %copy.63 = f32[1,4,40,2,6400]{4,2,1,3,0:T(8,128)} copy(f32[1,4,40,2,6400]{4,3,2,1,0:T(2,128)} %param.8) | data formatting | bytes 16384000 | tf_op args[0]
  18.1 15.0 %reshape_squeeze.3 = f32[4,40,2,80,80]{4,3,1,0,2:T(8,128)} reshape(f32[1,4,40,2,6400]{4,2,1,3,0:T(8,128)} %copy.63) | data formatting | bytes 16384000 | tf_op jit(solution)/shard_map/reshape;squeeze | solution.py:16
  33.6 6.6 %fusion.4 = f32[4,16,40,80]{3,1,2,0:T(8,128)} fusion(f32[4,40,2,80,80]{4,3,1,0,2:T(8,128)} %reshape_squeeze.3, f32[4,2,80,16]{2,3,1,0:T(8,128)S(1)} %gather_fusion), kind=kOutput, calls=%fused_computation.16 | convolution fusion | flops 196608000 | bytes 7405568 | tf_op jit(solution)/shard_map/smi,spmn->spin/dot_general | solution.py:24
  40.2 5.3 %fusion.5 = f32[4,16,40,80]{3,1,2,0:T(8,128)S(1)} fusion(f32[4,40,2,80,80]{4,3,1,0,2:T(8,128)} %reshape_squeeze.3, f32[4,2,80,16]{2,3,1,0:T(8,128)S(1)} %gather_fusion), kind=kOutput, calls=%fused_computation.17 | convolution fusion | flops 196608000 | bytes 7405568 | tf_op jit(solution)/shard_map/smi,spmn->spin/dot_general | solution.py:21
  45.5 3.2 fusion.9
  48.7 0.6 gather_fusion.1
  49.4 0.6 gather_fusion.2
  50.0 1.7 fusion.16
  51.7 1.7 fusion.14
  53.3 5.4 %fusion.11 = f32[4,40,16,80]{3,2,1,0:T(8,128)S(1)} fusion(f32[4,16,40,80]{3,1,2,0:T(8,128)S(1)} %copy-done.4, f32[4,40,2,80,80]{4,3,1,0,2:T(8,128)} %reshape_squeeze.3, f32[4,2,80,16]{2,3,1,0:T(8,128)S(1)} %gather_fusion), kind=kOutput, calls=%fused_computation.26 | convolution fusion | flops 196812800 | bytes 8716288 | tf_op jit(solution)/shard_map/smi,spmn->spin/dot_general | solution.py:24
  58.8 1.7 convolution_subtract_fusion
  60.5 1.7 convolution_add_fusion
  62.2 1.2 pad_maximum_fusion
  63.4 70.2 %all-gather.2.cloned.1.call-done = f32[2,640,16,128]{3,1,2,0:T(8,128)} async-done(((f32[2,40,16,128]{3,1,2,0:T(8,128)}), f32[2,640,16,128]{3,1,2,0:T(8,128)}) %all-gather.2.cloned.1.call-update) | async-done | bytes 10485776 | tf_op jit(solution)/shard_map/all_gather | solution.py:92
  133.6 1.2 collective-permute-start
  134.8 0.9 copy.71
  135.7 4.8 %all-to-all-start = ((f32[2,40,16,128]{3,1,0,2:T(8,128)}), f32[2,40,16,128]{3,1,0,2:T(8,128)S(1)}, u32[]{:S(2)}, u32[]{:S(2)}) async-start(f32[2,40,16,128]{3,1,0,2:T(8,128)} %copy.71), calls=%async_computation | async-start | bytes 1310720 | tf_op jit(solution)/shard_map/all_to_all | solution.py:84
  142.6 0.6 gather_fusion.6
  143.4 0.6 gather_fusion.3
  146.1 14.4 %all-to-all-done = f32[2,40,16,128]{3,1,0,2:T(8,128)S(1)} async-done(((f32[2,40,16,128]{3,1,0,2:T(8,128)}), f32[2,40,16,128]{3,1,0,2:T(8,128)S(1)}, u32[]{:S(2)}, u32[]{:S(2)}) %all-to-all-start) | async-done | bytes 655392 | tf_op jit(solution)/shard_map/all_to_all | solution.py:84
  160.6 200.1 %collective-permute-done = f32[2,640,16,128]{3,1,2,0:T(8,128)} collective-permute-done((f32[2,640,16,128]{3,1,2,0:T(8,128)}, f32[2,640,16,128]{3,1,2,0:T(8,128)}, u32[]{:S(2)}, u32[]{:S(2)}) %collective-permute-start) | collective-permute-done | bytes 10485792 | tf_op jit(solution)/shard_map/ppermute | solution.py:10
  360.7 22.3 %fusion.3 = f32[2,16,64,2,64]{4,2,3,1,0:T(8,128)S(1)} fusion(f32[2,640,16,128]{3,1,2,0:T(8,128)} %collective-permute-done, f32[2,640,1,128]{3,1,0,2:T(8,128)S(1)} %bitcast.149), kind=kOutput, calls=%fused_computation.13 | convolution fusion | flops 2013265920 | bytes 12189696 | tf_op jit(solution)/shard_map/spia,tpjb->stijab/dot_general | solution.py:45
  382.9 20.7 %subtract_divide_fusion.1 = f32[2,2,1,16,64,64]{4,5,0,3,1,2:T(8,128)} fusion(f32[2,16,64,2,64]{4,2,3,1,0:T(8,128)S(1)} %fusion.3, f32[2,640,16,128]{3,1,2,0:T(8,128)} %collective-permute-done, f32[2,64]{1,0:T(2,128)S(1)} %gather_fusion.7, f32[2,2,16,64]{3,0,2,1:T(2,128)S(1)} %broadcast_subtract_fusion, f32[2,640,1,128]{3,1,0,2:T(8,128)S(1)} %bitcast.150), kind=kOutput, calls=%fused_computation.21 | convolution fusion | flops 2014052352 | bytes 13255168 | tf_op jit(solution)/shard_map/spia,tpjb->stijab/dot_general | solution.py:45
  403.7 2.9 copy.79
  406.6 2.1 stack.9
  408.7 19.9 %fusion = f32[2,16,64,2,64]{4,2,3,1,0:T(8,128)S(1)} fusion(f32[2,640,16,128]{3,1,2,0:T(8,128)} %collective-permute-done, f32[2,640,1,128]{3,1,0,2:T(8,128)S(1)} %bitcast.151), kind=kOutput, calls=%fused_computation.10 | convolution fusion | flops 2013265920 | bytes 12189696 | tf_op jit(solution)/shard_map/spia,tpjb->stijab/dot_general | solution.py:48
  428.6 23.3 %subtract_divide_fusion = f32[2,2,1,16,64,64]{4,5,0,3,1,2:T(8,128)} fusion(f32[2,16,64,2,64]{4,2,3,1,0:T(8,128)S(1)} %fusion, f32[2,640,16,128]{3,1,2,0:T(8,128)} %collective-permute-done, f32[2,64]{1,0:T(2,128)S(1)} %gather_fusion.7, f32[2,2,16,64]{3,0,2,1:T(2,128)S(1)} %broadcast_subtract_fusion, f32[2,640,1,128]{3,1,0,2:T(8,128)S(1)} %bitcast.152), kind=kOutput, calls=%fused_computation.20 | convolution fusion | flops 2014052352 | bytes 13255168 | tf_op jit(solution)/shard_map/spia,tpjb->stijab/dot_general | solution.py:48
  451.9 2.9 copy.82
  454.9 3.0 stack.10
  457.9 2.7 maximum_bitcast_fusion
  (40 shorter events, 3.1 us)
Async XLA Ops:
  6.5 42.9 %copy-start = (f32[27,2,80,64]{2,3,1,0:T(8,128)S(1)}, f32[27,2,80,64]{2,3,1,0:T(8,128)}, u32[]{:S(2)}) copy-start(f32[27,2,80,64]{2,3,1,0:T(8,128)} %param.10) | copy-start | bytes 3317764
  6.5 127.1 %all-gather.2.cloned.1.call-start = ((), (), s32[]{:S(2)}) async-start(), calls=%async_computation.1 | async-start | bytes 11141120 | tf_op jit(solution)/shard_map/all_gather | solution.py:92
  18.1 15.0 %copy-start.5 = (f32[27,2,80,16]{2,3,1,0:T(8,128)S(1)}, f32[27,2,80,16]{2,3,1,0:T(8,128)}, u32[]{:S(2)}) copy-start(f32[27,2,80,16]{2,3,1,0:T(8,128)} %param.9) | copy-start | bytes 829444
  33.6 11.9 %copy-start.2 = (f32[4,40,2,80,80]{4,3,1,0,2:T(8,128)S(1)}, f32[4,40,2,80,80]{4,3,1,0,2:T(8,128)}, u32[]{:S(2)}) copy-start(f32[4,40,2,80,80]{4,3,1,0,2:T(8,128)} %reshape_squeeze.3) | copy-start | bytes 24576004
  45.5 3.2 copy-start.3
  50.0 3.3 copy-start.4
  63.4 79.9 %copy-start.7 = (f32[27,16]{0,1:T(8,128)S(1)}, f32[27,16]{0,1:T(8,128)}, u32[]{:S(2)}) copy-start(f32[27,16]{0,1:T(8,128)} %param.11) | copy-start | bytes 5188
  63.4 81.2 %copy-start.6 = (f32[27,64]{1,0:T(8,128)S(1)}, f32[27,64]{1,0:T(8,128)}, u32[]{:S(2)}) copy-start(f32[27,64]{1,0:T(8,128)} %param.12) | copy-start | bytes 20740
  133.6 227.1 %collective-permute-start = (f32[2,640,16,128]{3,1,2,0:T(8,128)}, f32[2,640,16,128]{3,1,2,0:T(8,128)}, u32[]{:S(2)}, u32[]{:S(2)}) collective-permute-start(f32[2,640,16,128]{3,1,2,0:T(8,128)} %all-gather.2.cloned.1.call-done), channel_id=1, source_target_pairs={{0,16},{16,0},{32,48},{48,32},{64,80},{80,64},{96,112},{112,96},{1... | collective-permute-start | bytes 31457288 | tf_op jit(solution)/shard_map/ppermute | solution.py:10
  135.7 24.8 %all-to-all-start = ((f32[2,40,16,128]{3,1,0,2:T(8,128)}), f32[2,40,16,128]{3,1,0,2:T(8,128)S(1)}, u32[]{:S(2)}, u32[]{:S(2)}) async-start(f32[2,40,16,128]{3,1,0,2:T(8,128)} %copy.71), calls=%async_computation | async-start | bytes 1310720 | tf_op jit(solution)/shard_map/all_to_all | solution.py:84
  454.9 5.7 %copy-start.1 = (f32[27,2,80,64]{2,3,1,0:T(8,128)S(1)}, f32[27,2,80,64]{2,3,1,0:T(8,128)}, u32[]{:S(2)}) copy-start(f32[27,2,80,64]{2,3,1,0:T(8,128)} %param.10) | copy-start | bytes 3317764
Sparse Core Ops, SparseCore 0:
  63.6 69.9 all-gather.1
where the time goes:
time: 477 us; the launch traced here: 468 us
  waiting for transfers between devices  285 us (60%)
  matrix products  113 us (24%)
  local copies, waits for them, and re-layouts  41.6 us (9%)
  between operations  17.6 us (4%)
  starting transfers between devices  6.02 us (1%)
    ppermute x1, waiting for transfers between devices, partner_2(): return lax.ppermute(value, axis, pairs)  200 us
    all_gather x1, waiting for transfers between devices, per_device(): gathered = lax.all_gather(jb_side, 'aux', axis=1, tiled=True)  70.2 us
    dot_general x1, matrix products, pair_sums(): jnp.einsum(pattern, left_real, right_imag, precision=highest)  23.3 us
    dot_general x1, matrix products, pair_sums(): jnp.einsum(pattern, left_imag, right_imag, precision=highest)  22.3 us
    dot_general x1, matrix products, pair_sums(): jnp.einsum(pattern, left_real, right_real, precision=highest)  20.7 us
    dot_general x1, matrix products, pair_sums(): jnp.einsum(pattern, left_imag, right_real, precision=highest)  19.9 us
    another operation x1, local copies, waits for them, and re-layouts, to_orbitals(): blocks.reshape(blocks.shape[0], blocks.shape[1], 2, ao_width, ao_width)  15 us
    all_to_all x1, waiting for transfers between devices, per_device(): lax.all_to_all(own_orbitals[0:2], 'aux', split_axis=2, concat_axis=1, til...  14.4 us
  transfers between devices with their start and end apart: 3, of which 3 were waited for; matrix products, arithmetic and copies ran while one was open for 1% of the time, Pallas kernels for 0%

commit v1 on v0

v1 whole, which is shorter than its diff:
```python
import functools

import jax
import jax.numpy as jnp
from jax import lax
from jax.experimental import pallas as pl
from jax.experimental.pallas import tpu as pltpu
from jax.sharding import PartitionSpec as P

MESH = pl.DeviceIdType.MESH
F32 = jnp.float32
BF16 = jnp.bfloat16

TILES = tuple(
    tuple((m, 80 * m - 128 * k) for m in range(8) if -80 < 80 * m - 128 * k < 128)
    for k in range(5)
)


def halves(x):
    hi = x.astype(BF16)
    return hi, (x - hi.astype(F32)).astype(BF16)


def dot(x, y):
    return jnp.dot(x, y, preferred_element_type=F32)


def swap_sides(x):
    return pltpu.roll(x, 64, 1)


def fill_weights(vir_ref, w_hi, w_lo):
    vre, vim = vir_ref[0, 0], vir_ref[0, 1]
    pad = jnp.zeros((128, 48), F32)
    for part, top, bottom in ((0, vre, vim), (1, -vim, vre)):
        stacked = jnp.concatenate([jnp.concatenate([top, bottom], 0), pad], 1)
        hi, lo = halves(stacked.T[:80])
        for k, blocks in enumerate(TILES):
            for b, (_, start) in enumerate(blocks):
                first, last = max(start, 0), min(start + 80, 128)
                to = (k, slice(part * 128 + first, part * 128 + last), slice(128 * b, 128 * b + 128))
                w_hi[to] = hi[first - start : last - start]
                w_lo[to] = lo[first - start : last - start]


def orbitals(s, ao_ref, occ_ref, vir_ref, put, w_hi, w_lo, x_hi, x_lo, t1):
    fill_weights(vir_ref, w_hi, w_lo)

    def load(pair, _):
        for k in range(5):
            sides = []
            for part in range(2):
                sides.append(
                    jnp.concatenate(
                        [
                            ao_ref[0, pl.ds(((pair * 2 + h) * 5 + k) * 2 + part, 40, stride=100), :]
                            for h in range(2)
                        ],
                        0,
                    )
                )
            hi, lo = halves(jnp.concatenate(sides, 1))
            at = pl.ds(pl.multiple_of(pair * 80, 16), 80)
            x_hi[k, at, :] = hi
            x_lo[k, at, :] = lo
        return 0

    lax.fori_loop(0, 5, load, 0)
    carry = None
    for k, blocks in enumerate(TILES):
        width = 128 * len(blocks)
        wh, wl = w_hi[k, :, :width], w_lo[k, :, :width]
        xh, xl = x_hi[k], x_lo[k]
        y = dot(xh, wh) + dot(xh, wl) + dot(xl, wh)
        for b, (m, start) in enumerate(blocks):
            value = y[:, 128 * b : 128 * b + 128]
            if start < 0:
                value = value + carry
            if start + 80 > 128:
                carry = value
                continue
            for g in range(10):
                t1[pl.ds(8 * g + m, 40, stride=80), :] = value[40 * g : 40 * g + 40]

    occ = jnp.concatenate([occ_ref[0, 0], occ_ref[0, 1]], 0)
    c_hi, c_lo = halves(occ)
    c_both = jnp.concatenate([c_hi, c_lo], 0)
    sign = jnp.where(lax.broadcasted_iota(jnp.int32, (16, 128), 1) < 64, 1.0, -1.0).astype(F32)

    def second(pair, _):
        rows = t1[pl.ds(pl.multiple_of(pair * 160, 8), 160), :]
        hi, lo = halves(jnp.concatenate([rows[:80], rows[80:]], 1))
        both = dot(c_both, hi)
        u = both[:32] + both[32:] + dot(c_hi, lo)
        for h in range(2):
            ure, uim = u[:16, 128 * h : 128 * h + 128], u[16:, 128 * h : 128 * h + 128]
            put(pair * 2 + h, ure + sign * swap_sides(uim))
        return 0

    lax.fori_loop(0, 20, second, 0, unroll=4)


def step_one_kernel(
    place, rows, diff, label, ao_ref, occ_ref, vir_ref, occ_e, vir_e, lr_ref, base_ref, occr_ref,
    w_hi, w_lo, x_hi, x_lo, t1,
):
    s = pl.program_id(0)

    @pl.when(s == 0)
    def _():
        w_hi[...] = jnp.zeros_like(w_hi)
        w_lo[...] = jnp.zeros_like(w_lo)
        slot, i = place[0], place[1]
        other = slot + 1 - 2 * (slot % 2)
        col = lax.broadcasted_iota(jnp.int32, (32, 64), 1)
        row = lax.broadcasted_iota(jnp.int32, (32, 64), 0)
        low = lax.broadcasted_iota(jnp.int32, (32, 128), 1) < 64
        lane = lax.broadcasted_iota(jnp.int32, (1, 16), 1)
        eye = lax.broadcasted_iota(jnp.int32, (16, 16), 0) == lax.broadcasted_iota(jnp.int32, (16, 16), 1)
        for b in range(2):
            ki = rows[slot, b]
            ka = diff[ki, label[slot]]
            occ_left = jnp.sum(jnp.where(lane == i, occ_e[pl.ds(ki, 1), :], 0.0), axis=1, keepdims=True)
            line = vir_e[pl.ds(ka, 1), :]
            even = jnp.sum(jnp.where(col == 2 * row, line, 0.0), axis=1, keepdims=True)
            odd = jnp.sum(jnp.where(col == 2 * row + 1, line, 0.0), axis=1, keepdims=True)
            left = occ_left - jnp.where(low, even, odd)
            for t in range(2):
                kj = rows[other, 2 + t]
                kb = diff[kj, label[other]]
                right = vir_e[pl.ds(kb, 1), :]
                base_ref[2 * b + t] = left - jnp.concatenate([right, right], 1)
                if b == 0:
                    occ_right = jnp.sum(jnp.where(eye, occ_e[pl.ds(kj, 1), :], 0.0), axis=1, keepdims=True)
                    occr_ref[t] = jnp.broadcast_to(occ_right, (16, 128))

    def put(p, value):
        lr_ref[pl.ds(s * 640 + p, 16, stride=40), :] = value

    orbitals(s, ao_ref, occ_ref, vir_ref, put, w_hi, w_lo, x_hi, x_lo, t1)


def step_one(place, rows, diff, label, ao, occ, vir, occ_e, vir_e):
    def k_of(s, place, rows, diff, label):
        return rows[place[0], s]

    def occ_at(s, *scalars):
        return (k_of(s, *scalars), 0, 0, 0)

    def vir_at(s, place, rows, diff, label):
        return (diff[rows[place[0], s], label[place[0]]], 0, 0, 0)

    def whole(*shape):
        return pl.BlockSpec(shape, lambda s, *_: (0,) * len(shape))

    return pl.pallas_call(
        step_one_kernel,
        out_shape=(
            jax.ShapeDtypeStruct((2560, 128), F32),
            jax.ShapeDtypeStruct((4, 32, 128), F32),
            jax.ShapeDtypeStruct((2, 16, 128), F32),
        ),
        grid_spec=pltpu.PrefetchScalarGridSpec(
            num_scalar_prefetch=4,
            grid=(4,),
            in_specs=[
                pl.BlockSpec((1, 4000, 128), lambda s, *_: (s, 0, 0)),
                pl.BlockSpec((1, 2, 16, 80), occ_at),
                pl.BlockSpec((1, 2, 64, 80), vir_at),
                whole(27, 16),
                whole(27, 64),
            ],
            out_specs=(whole(2560, 128), whole(4, 32, 128), whole(2, 16, 128)),
            scratch_shapes=[
                pltpu.VMEM((5, 256, 384), BF16),
                pltpu.VMEM((5, 256, 384), BF16),
                pltpu.VMEM((5, 400, 256), BF16),
                pltpu.VMEM((5, 400, 256), BF16),
                pltpu.VMEM((3200, 128), F32),
            ],
        ),
        compiler_params=pltpu.CompilerParams(vmem_limit_bytes=40 * 2**20),
        cost_estimate=pl.CostEstimate(flops=2 * 10**9, bytes_accessed=9 * 10**6, transcendentals=0),
        name="step_one",
    )(place, rows, diff, label, ao, occ, vir, occ_e, vir_e)


POS = {0: 0, 1: 1, -1: 2, 2: 3, -2: 4, 3: 5, -3: 6, 4: 7, -4: 7}
STAGES = ((0, 240), (240, 400), (400, 640))


def pair_kernel(
    lr_ref, base_ref, occr_ref, out_ref, rbuf, lbuf, lt_hi, lt_lo, ybuf,
    par_send, par_recv, hop_send, hop_recv, sib_send, sib_recv, l_send, l_recv, own_sem,
):
    pb, aux = lax.axis_index("pb"), lax.axis_index("aux")
    z, c = aux // 2, aux % 2
    partner = pb + 1 - 2 * (pb % 2)
    sibling = aux + 1 - 2 * c

    def at_z(dz, core):
        return lax.rem(z + dz + 8, 8) * 2 + core

    barrier = pltpu.get_barrier_semaphore()
    for far in range(1, 16):
        pl.semaphore_signal(barrier, inc=1, device_id={"aux": lax.rem(aux + far, 16)}, device_id_type=MESH)
    pl.semaphore_signal(barrier, inc=1, device_id={"pb": partner}, device_id_type=MESH)
    pl.semaphore_wait(barrier, 16)

    def place(pos, core):
        return pl.ds(pl.multiple_of(pos * 80 + core * 40, 8), 40)

    def chunk(pos, t):
        return rbuf.at[pl.ds(16 * t, 16), place(pos, c), :]

    def partner_copy(t):
        return pltpu.make_async_remote_copy(
            lr_ref.at[2 + t], chunk(0, t), par_send.at[t], par_recv.at[t],
            device_id={"pb": partner}, device_id_type=MESH,
        )

    def hop_copy(way, d, t):
        step = 1 - 2 * way
        return pltpu.make_async_remote_copy(
            chunk(POS[-step * (d - 1)], t), chunk(POS[-step * d], t),
            hop_send.at[way, d - 1, t], hop_recv.at[way, d - 1, t],
            device_id={"aux": at_z(step, c)}, device_id_type=MESH,
        )

    def sibling_copy(pos, t):
        return pltpu.make_async_remote_copy(
            chunk(pos, t), chunk(pos, t), sib_send.at[pos, t], sib_recv.at[pos, t],
            device_id={"aux": sibling}, device_id_type=MESH,
        )

    def row_copy(dz, cross):
        core = c + cross * (1 - 2 * c)
        to = at_z(dz, core)
        pos = POS[-dz]
        src, dst = lr_ref.at[pl.ds(0, 2), to], lbuf.at[:, place(pos, c), :]
        if dz == 0 and cross == 0:
            return pltpu.make_async_copy(src, dst, own_sem)
        return pltpu.make_async_remote_copy(
            src, dst, l_send.at[pos, cross], l_recv.at[pos, cross],
            device_id={"aux": to}, device_id_type=MESH,
        )

    def has_hop(way, d, t):
        return d < 4 or t == way

    partners = [partner_copy(t) for t in range(2)]
    for copy in partners:
        copy.start()
    rows = {(dz, cross): row_copy(dz, cross) for dz in (4, 3, -3, 2, -2, 1, -1, 0) for cross in range(2)}
    for copy in rows.values():
        copy.start()

    sent = []

    def send(copy):
        copy.start()
        sent.append(copy)

    for t in range(2):
        partners[t].wait_recv()
        for way in range(2):
            send(hop_copy(way, 1, t))
        send(sibling_copy(0, t))

    def relay(d):
        for t in range(2):
            for way in range(2):
                if not has_hop(way, d, t):
                    continue
                hop_copy(way, d, t).wait_recv()
                if d < 4 and has_hop(way, d + 1, t):
                    send(hop_copy(way, d + 1, t))
                send(sibling_copy(POS[-d if way == 0 else d], t))

    def left_sides():
        for (dz, cross), copy in rows.items():
            if dz == 0 and cross == 0:
                copy.wait()
            else:
                copy.wait_recv()
        for n, (first, last) in enumerate(STAGES):
            for s in range(2):
                part = lbuf[s, first:last, :]
                part = jnp.concatenate([part, jnp.zeros((256 - (last - first), 128), F32)], 0)
                hi, lo = halves(part.T)
                lt_hi[n, 128 * s : 128 * s + 128, :] = hi
                lt_lo[n, 128 * s : 128 * s + 128, :] = lo

    low = lax.broadcasted_iota(jnp.int32, (32, 128), 1) < 64

    def finish(n):
        t, j = n // 16, n % 16
        for s in range(2):
            def half(part, odd):
                return ybuf[n, pl.ds(128 * s + 64 * part + odd, 32, stride=2), :]

            re_e, re_d, im_e, im_d = half(0, 0), half(0, 1), half(1, 0), half(1, 1)
            inverse = 1.0 / (base_ref[2 * s + t] + occr_ref[t, pl.ds(j, 1), :])
            real = jnp.where(low, re_e, swap_sides(re_d)) - jnp.where(low, swap_sides(im_e), im_d)
            imag = jnp.where(low, swap_sides(re_e), re_d) + jnp.where(low, im_e, swap_sides(im_d))
            for part, value in enumerate((real, imag)):
                first = ((part * 2 + s) * 2 + t) * 512 + (j // 8) * 256 + j % 8
                out_ref[pl.ds(first, 32, stride=8), :] = value * inverse

    def multiply(stage):
        first, last = STAGES[stage]
        width = last - first

        def body(pair, _):
            r = jnp.concatenate([rbuf[pair * 2 + h, first:last, :] for h in range(2)], 1)
            hi, lo = halves(r)
            lh, ll = lt_hi[stage, :, :width], lt_lo[stage, :, :width]
            y = dot(lh, hi) + dot(ll, hi) + dot(lh, lo)
            for h in range(2):
                value = y[:, 128 * h : 128 * h + 128]
                if stage > 0:
                    value = value + ybuf[pair * 2 + h]
                ybuf[pair * 2 + h] = value
                if stage == 2:
                    finish(pair * 2 + h)
            return 0

        lax.fori_loop(0, 16, body, 0)

    def from_sibling(*positions):
        for pos in positions:
            for t in range(2):
                sibling_copy(pos, t).wait_recv()

    relay(1)
    left_sides()
    from_sibling(0, 1, 2)
    relay(2)
    multiply(0)
    relay(3)
    from_sibling(3, 4)
    multiply(1)
    relay(4)
    from_sibling(5, 6, 7)
    multiply(2)
    for copy in partners + sent:
        copy.wait_send()
    for (dz, cross), copy in rows.items():
        if dz != 0 or cross != 0:
            copy.wait_send()


def pair_sums(lr, base, occr):
    vmem = pl.BlockSpec(memory_space=pltpu.VMEM)
    dma = pltpu.SemaphoreType.DMA
    return pl.pallas_call(
        pair_kernel,
        out_shape=jax.ShapeDtypeStruct((4096, 128), F32),
        in_specs=[pl.BlockSpec(memory_space=pl.ANY), vmem, vmem],
        out_specs=vmem,
        scratch_shapes=[
            pltpu.VMEM((32, 640, 128), F32),
            pltpu.VMEM((2, 640, 128), F32),
            pltpu.VMEM((3, 256, 256), BF16),
            pltpu.VMEM((3, 256, 256), BF16),
            pltpu.VMEM((32, 256, 128), F32),
            dma((2,)), dma((2,)),
            dma((2, 4, 2)), dma((2, 4, 2)),
            dma((8, 2)), dma((8, 2)),
            dma((8, 2)), dma((8, 2)),
            dma,
        ],
        compiler_params=pltpu.CompilerParams(
            collective_id=0, has_side_effects=True, vmem_limit_bytes=48 * 2**20
        ),
        cost_estimate=pl.CostEstimate(flops=4 * 10**9, bytes_accessed=4 * 10**6, transcendentals=0),
        name="pair_sums",
    )(lr, base, occr)


def per_device(
    ao_blocks, occ_coef, vir_coef, occ_energy, vir_energy, kpoint_diff, transfer_label, chosen_rows
):
    place = jnp.stack([lax.axis_index("pb"), lax.axis_index("aux")]).astype(jnp.int32)
    ao = ao_blocks.reshape(4, 40, 2, 50, 128).transpose(0, 1, 3, 2, 4).reshape(4, 4000, 128)
    lr, base, occr = step_one(
        place, chosen_rows, kpoint_diff, transfer_label, ao,
        occ_coef.swapaxes(2, 3), vir_coef.swapaxes(2, 3), occ_energy, vir_energy,
    )
    out = pair_sums(lr.reshape(4, 16, 40, 128), base, occr)
    out = out.reshape(2, 2, 2, 2, 32, 8, 128).transpose(0, 1, 2, 3, 5, 4, 6)
    return out.reshape(1, 2, 2, 2, 1, 16, 4096)


def solution(mesh):
    in_specs = (P("pb", None, "aux", None, None), P(), P(), P(), P(), P(), P(), P())
    out_specs = P("pb", None, None, None, "aux", None, None)
    return jax.shard_map(
        per_device, mesh=mesh, in_specs=in_specs, out_specs=out_specs, check_vma=False
    )
```

time: 477 us -> 129 us (0.27); the launches traced: 468 us -> 128 us
  waiting for transfers between devices: 285 us -> 0 us
  matrix products: 113 us -> 0 us
  Pallas kernels: 0 us -> 98.6 us
  between operations: 17.6 us -> 0.08 us
  local copies, waits for them, and re-layouts: 41.6 us -> 29.7 us
  starting transfers between devices: 6.02 us -> 0 us
    ppermute x1 -> x0, waiting for transfers between devices: 200 us -> none  [partner_2(): return lax.ppermute(value, axis, pairs)]
    dot_general x12 -> x0, matrix products: 113 us -> none  [the longest x1 23.3 us: pair_sums(): jnp.einsum(pattern, left_real, right_imag, precision=highest)]
    pallas_call x0 -> x2, Pallas kernels: none -> 98.6 us  [the longest x1 84.4 us: pair_sums(): pl.pallas_call(pair_kernel, out_shape=jax.ShapeDtypeStruct((4096, 128), F...]
    all_gather x1 -> x0, waiting for transfers between devices: 70.2 us -> none  [per_device(): gathered = lax.all_gather(jb_side, 'aux', axis=1, tiled=True)]
    another operation x3 -> x0, local copies, waits for them, and re-layouts: 20.2 us -> none  [the longest x1 15 us: to_orbitals(): blocks.reshape(blocks.shape[0], blocks.shape[1], 2, ao_width, ao_width)]
    all_to_all x1 -> x0, waiting for transfers between devices: 14.4 us -> none  [per_device(): lax.all_to_all(own_orbitals[0:2], 'aux', split_axis=2, concat_axis=1, til...]
    transpose x0 -> x1, local copies, waits for them, and re-layouts: none -> 13.1 us  [per_device(): ao_blocks.reshape(4, 40, 2, 50, 128).transpose(0, 1, 3, 2, 4)]
    reshape x0 -> x1, local copies, waits for them, and re-layouts: none -> 11.8 us  [per_device(): ao_blocks.reshape(4, 40, 2, 50, 128).transpose(0, 1, 3, 2, 4)]
  transfers between devices with their start and end apart: 3 -> 0, of which waited for: 3 -> 0; matrix products, arithmetic and copies ran while one was open for 1% -> 0% of each run, Pallas kernels for 0% -> 0%
where the time goes in v1:
time: 129 us; the launch traced here: 128 us
  Pallas kernels  98.6 us (76%)
  local copies, waits for them, and re-layouts  29.7 us (23%)
    pallas_call x1, Pallas kernels, pair_sums(): pl.pallas_call(pair_kernel, out_shape=jax.ShapeDtypeStruct((4096, 128), F...  84.4 us
    pallas_call x1, Pallas kernels, step_one(): pl.pallas_call(step_one_kernel, out_shape=(jax.ShapeDtypeStruct((2560, 12...  14.2 us
    transpose x1, local copies, waits for them, and re-layouts, per_device(): ao_blocks.reshape(4, 40, 2, 50, 128).transpose(0, 1, 3, 2, 4)  13.1 us
    reshape x1, local copies, waits for them, and re-layouts, per_device(): ao_blocks.reshape(4, 40, 2, 50, 128).transpose(0, 1, 3, 2, 4)  11.8 us
    unnamed x19, local copies, waits for them, and re-layouts  4.84 us

profile of v1, /device:TPU:1, one launch (start us, length us, event | category | flops | bytes accessed | tf_op | source)
XLA Modules:
  0.0 128.4 jit_solution(15002116583926822152)
XLA Ops:
  0.0 0.1 pad_add_fusion.place
  0.1 11.8 %reshape.20 = f32[4,40,2,50,128]{4,3,2,1,0:T(8,128)} reshape(f32[1,4,40,2,6400]{4,3,2,1,0:T(2,128)} %param.8) | data formatting | bytes 16384000 | tf_op jit(solution)/shard_map/reshape | solution.py:386
  11.8 0.0 copy-start.6
  11.8 0.0 copy-start.7
  11.9 0.0 copy-start.1
  11.9 0.0 copy-start.2
  11.9 0.0 copy-start.3
  11.9 0.0 copy-start.4
  11.9 0.0 copy-start.5
  11.9 13.1 %copy.13 = f32[4,40,50,2,128]{4,3,2,1,0:T(2,128)} copy(f32[4,40,50,2,128]{4,2,3,1,0:T(8,128)} %bitcast.18) | data formatting | bytes 16384000 | tf_op jit(solution)/shard_map/transpose | solution.py:386
  25.0 0.0 copy-done.6
  25.0 0.1 copy.15.occ_e
  25.1 0.0 copy-done.7
  25.1 0.1 copy.14.rows
  25.2 0.0 copy-done.1
  25.2 0.0 copy-done.2
  25.2 0.0 copy-done.3
  25.2 0.0 copy-done.4
  25.2 0.0 copy-done.5
  25.2 0.0 copy-start
  25.2 3.3 %copy-done = f32[4,40,50,2,128]{4,3,2,1,0:T(2,128)S(1)} copy-done((f32[4,40,50,2,128]{4,3,2,1,0:T(2,128)S(1)}, f32[4,40,50,2,128]{4,3,2,1,0:T(2,128)}, u32[]{:S(2)}) %copy-start) | copy-done | bytes 8192024
  28.6 14.2 %step_one.1 = (f32[2560,128]{1,0:T(8,128)S(1)}, f32[4,32,128]{2,1,0:T(8,128)S(1)}, f32[2,16,128]{2,1,0:T(8,128)S(1)}) custom-call(s32[2]{0:T(128)S(1)} %pad_add_fusion.place, s32[16,4]{1,0:T(8,128)S(1)} %copy.14.rows, s32[27,27]{1,0:T(8,128)S(1)} %copy-done.3, s32[16]{0:T(128)S(1)} %copy-done.5, f32[4,4000,128]{2,1,0:T(8,128)S(1)} %bitcast.13, ...), custom_call_target="tpu_custom_call" | custom-call | flops 2000000000 | bytes 9000000 | tf_op jit(solution)/shard_map/step_one/pallas_call | solution.py:157
  42.7 84.4 %pair_sums.1 = f32[4096,128]{1,0:T(8,128)S(1)} custom-call(f32[4,16,40,128]{3,2,1,0:T(8,128)S(1)} %bitcast.17, f32[4,32,128]{2,1,0:T(8,128)S(1)} %get-tuple-element.9.base_ref, f32[2,16,128]{2,1,0:T(8,128)S(1)} %get-tuple-element.10.occr_ref), custom_call_target="tpu_custom_call" | custom-call | flops 4000000000 | bytes 4000000 | tf_op jit(solution)/shard_map/pair_sums/pallas_call | solution.py:357
  127.1 1.3 %copy.19 = f32[1,2,2,2,1,16,4096]{6,5,4,3,2,1,0:T(8,128)} copy(f32[1,2,2,2,1,16,4096]{6,5,4,3,2,1,0:T(8,128)S(1)} %bitcast.14) | data formatting | bytes 4194304
Async XLA Ops:
  11.8 13.2 %copy-start.6 = (f32[27,16]{0,1:T(8,128)S(1)}, f32[27,16]{0,1:T(8,128)}, u32[]{:S(2)}) copy-start(f32[27,16]{0,1:T(8,128)} %param.11) | copy-start | bytes 5188
  11.8 13.3 %copy-start.7 = (s32[16,4]{0,1:T(4,128)S(1)}, s32[16,4]{0,1:T(4,128)}, u32[]{:S(2)}) copy-start(s32[16,4]{0,1:T(4,128)} %param.15) | copy-start | bytes 772
  11.9 13.3 %copy-start.1 = (f32[27,2,80,64]{2,3,1,0:T(8,128)S(1)}, f32[27,2,80,64]{2,3,1,0:T(8,128)}, u32[]{:S(2)}) copy-start(f32[27,2,80,64]{2,3,1,0:T(8,128)} %param.10) | copy-start | bytes 3317764
  11.9 13.3 %copy-start.2 = (f32[27,2,80,16]{2,3,1,0:T(8,128)S(1)}, f32[27,2,80,16]{2,3,1,0:T(8,128)}, u32[]{:S(2)}) copy-start(f32[27,2,80,16]{2,3,1,0:T(8,128)} %param.9) | copy-start | bytes 829444
  11.9 13.3 %copy-start.3 = (s32[27,27]{1,0:T(8,128)S(1)}, s32[27,27]{1,0:T(8,128)}, u32[]{:S(2)}) copy-start(s32[27,27]{1,0:T(8,128)} %diff.1) | copy-start | bytes 8752
  11.9 13.3 %copy-start.4 = (f32[27,64]{1,0:T(8,128)S(1)}, f32[27,64]{1,0:T(8,128)}, u32[]{:S(2)}) copy-start(f32[27,64]{1,0:T(8,128)} %vir_e.1) | copy-start | bytes 20740
  11.9 13.3 %copy-start.5 = (s32[16]{0:T(128)S(1)}, s32[16]{0:T(128)}, u32[]{:S(2)}) copy-start(s32[16]{0:T(128)} %label.1) | copy-start | bytes 196
  25.2 3.3 %copy-start = (f32[4,40,50,2,128]{4,3,2,1,0:T(2,128)S(1)}, f32[4,40,50,2,128]{4,3,2,1,0:T(2,128)}, u32[]{:S(2)}) copy-start(f32[4,40,50,2,128]{4,3,2,1,0:T(2,128)} %copy.13) | copy-start | bytes 24576004

commit v2 on v1

--- a/solution.py
+++ b/solution.py
@@ -4,6 +4,7 @@
 import jax.numpy as jnp
 from jax import lax
 from jax.experimental import pallas as pl
+from jax.experimental.layout import Layout, with_layout_constraint
 from jax.experimental.pallas import tpu as pltpu
 from jax.sharding import PartitionSpec as P
 
@@ -383,7 +384,10 @@
     ao_blocks, occ_coef, vir_coef, occ_energy, vir_energy, kpoint_diff, transfer_label, chosen_rows
 ):
     place = jnp.stack([lax.axis_index("pb"), lax.axis_index("aux")]).astype(jnp.int32)
-    ao = ao_blocks.reshape(4, 40, 2, 50, 128).transpose(0, 1, 3, 2, 4).reshape(4, 4000, 128)
+    ao = with_layout_constraint(
+        ao_blocks.reshape(4, 40, 2, 50, 128), Layout(major_to_minor=(0, 1, 3, 2, 4))
+    )
+    ao = ao.transpose(0, 1, 3, 2, 4).reshape(4, 4000, 128)
     lr, base, occr = step_one(
         place, chosen_rows, kpoint_diff, transfer_label, ao,
         occ_coef.swapaxes(2, 3), vir_coef.swapaxes(2, 3), occ_energy, vir_energy,

time: 129 us -> 110 us (0.85)
  local copies, waits for them, and re-layouts: 29.7 us -> 10.8 us
    transpose x1 -> x0, local copies, waits for them, and re-layouts: 13.1 us -> none  [per_device(): ao_blocks.reshape(4, 40, 2, 50, 128).transpose(0, 1, 3, 2, 4)]
    reshape x1 -> x0, local copies, waits for them, and re-layouts: 11.8 us -> none  [per_device(): ao_blocks.reshape(4, 40, 2, 50, 128).transpose(0, 1, 3, 2, 4)]
    unnamed x19 -> x15, local copies, waits for them, and re-layouts: 4.84 us -> 10.8 us
where the time goes in v2:
time: 110 us; the launch traced here: 109 us
  Pallas kernels  98.6 us (90%)
  local copies, waits for them, and re-layouts  10.8 us (10%)
    pallas_call x1, Pallas kernels, pair_sums(): pl.pallas_call(pair_kernel, out_shape=jax.ShapeDtypeStruct((4096, 128), F...  84.4 us
    pallas_call x1, Pallas kernels, step_one(): pl.pallas_call(step_one_kernel, out_shape=(jax.ShapeDtypeStruct((2560, 12...  14.2 us
    unnamed x15, local copies, waits for them, and re-layouts  10.8 us

profile of v2, /device:TPU:1, one launch (start us, length us, event | category | flops | bytes accessed | tf_op | source)
XLA Modules:
  0.0 109.4 jit_solution(5371257623876148792)
XLA Ops:
  0.0 0.1 pad_add_fusion.place
  0.1 0.8 copy.9.rows
  0.8 0.8 copy.10.occ_e
  1.6 0.0 copy-start
  1.6 3.3 %copy-done = f32[1,4,40,2,6400]{4,3,2,1,0:T(2,128)S(1)} copy-done((f32[1,4,40,2,6400]{4,3,2,1,0:T(2,128)S(1)}, f32[1,4,40,2,6400]{4,3,2,1,0:T(2,128)}, u32[]{:S(2)}) %copy-start) | copy-done | bytes 8192024
  4.9 0.0 copy-start.1
  4.9 1.5 %copy-done.1 = f32[27,2,80,64]{2,3,1,0:T(8,128)S(1)} copy-done((f32[27,2,80,64]{2,3,1,0:T(8,128)S(1)}, f32[27,2,80,64]{2,3,1,0:T(8,128)}, u32[]{:S(2)}) %copy-start.1) | copy-done | bytes 1105944
  6.4 0.0 copy-start.2
  6.4 1.0 copy-done.2
  7.4 0.0 copy-start.3
  7.4 0.7 copy-done.3
  8.2 0.0 copy-start.4
  8.2 0.7 copy-done.4
  8.9 0.0 copy-start.5
  8.9 0.7 copy-done.5
  9.5 14.2 %step_one.1 = (f32[2560,128]{1,0:T(8,128)S(1)}, f32[4,32,128]{2,1,0:T(8,128)S(1)}, f32[2,16,128]{2,1,0:T(8,128)S(1)}) custom-call(s32[2]{0:T(128)S(1)} %pad_add_fusion.place, s32[16,4]{1,0:T(8,128)S(1)} %copy.9.rows, s32[27,27]{1,0:T(8,128)S(1)} %copy-done.3, s32[16]{0:T(128)S(1)} %copy-done.5, f32[4,4000,128]{2,1,0:T(8,128)S(1)} %bitcast.15, ...), custom_call_target="tpu_custom_call" | custom-call | flops 2000000000 | bytes 9000000 | tf_op jit(solution)/shard_map/step_one/pallas_call | solution.py:158
  23.7 84.4 %pair_sums.1 = f32[4096,128]{1,0:T(8,128)S(1)} custom-call(f32[4,16,40,128]{3,2,1,0:T(8,128)S(1)} %bitcast.19, f32[4,32,128]{2,1,0:T(8,128)S(1)} %get-tuple-element.9.base_ref, f32[2,16,128]{2,1,0:T(8,128)S(1)} %get-tuple-element.10.occr_ref), custom_call_target="tpu_custom_call" | custom-call | flops 4000000000 | bytes 4000000 | tf_op jit(solution)/shard_map/pair_sums/pallas_call | solution.py:358
  108.1 1.3 %copy.12 = f32[1,2,2,2,1,16,4096]{6,5,4,3,2,1,0:T(8,128)} copy(f32[1,2,2,2,1,16,4096]{6,5,4,3,2,1,0:T(8,128)S(1)} %bitcast.16) | data formatting | bytes 4194304
Async XLA Ops:
  1.6 3.3 %copy-start = (f32[1,4,40,2,6400]{4,3,2,1,0:T(2,128)S(1)}, f32[1,4,40,2,6400]{4,3,2,1,0:T(2,128)}, u32[]{:S(2)}) copy-start(f32[1,4,40,2,6400]{4,3,2,1,0:T(2,128)} %param.8) | copy-start | bytes 24576004
  4.9 1.5 %copy-start.1 = (f32[27,2,80,64]{2,3,1,0:T(8,128)S(1)}, f32[27,2,80,64]{2,3,1,0:T(8,128)}, u32[]{:S(2)}) copy-start(f32[27,2,80,64]{2,3,1,0:T(8,128)} %param.10) | copy-start | bytes 3317764
  6.4 1.0 copy-start.2
  7.4 0.7 copy-start.3
  8.2 0.7 copy-start.4
  8.9 0.7 copy-start.5

commit v3 on v2

v3 whole, which is shorter than its diff:
```python
import functools

import jax
import jax.numpy as jnp
from jax import lax
from jax.experimental import pallas as pl
from jax.experimental.layout import Layout, with_layout_constraint
from jax.experimental.pallas import tpu as pltpu
from jax.sharding import PartitionSpec as P

MESH = pl.DeviceIdType.MESH
F32 = jnp.float32
BF16 = jnp.bfloat16

TILES = tuple(
    tuple((m, 80 * m - 128 * k) for m in range(8) if -80 < 80 * m - 128 * k < 128)
    for k in range(5)
)


def halves(x):
    hi = x.astype(BF16)
    return hi, (x - hi.astype(F32)).astype(BF16)


def dot(x, y):
    return jnp.dot(x, y, preferred_element_type=F32)


def swap_sides(x):
    return pltpu.roll(x, 64, 1)


def fill_weights(vir_ref, s, w_hi, w_lo):
    vre, vim = vir_ref[s, 0], vir_ref[s, 1]
    pad = jnp.zeros((128, 48), F32)
    for part, top, bottom in ((0, vre, vim), (1, -vim, vre)):
        stacked = jnp.concatenate([jnp.concatenate([top, bottom], 0), pad], 1)
        hi, lo = halves(stacked.T[:80])
        for k, blocks in enumerate(TILES):
            for b, (_, start) in enumerate(blocks):
                first, last = max(start, 0), min(start + 80, 128)
                to = (k, slice(part * 128 + first, part * 128 + last), slice(128 * b, 128 * b + 128))
                w_hi[to] = hi[first - start : last - start]
                w_lo[to] = lo[first - start : last - start]


def orbitals(s, ao_ref, occ_ref, vir_ref, put, w_hi, w_lo, x_hi, x_lo, t1):
    fill_weights(vir_ref, s, w_hi, w_lo)

    def load(pair, _):
        for k in range(5):
            sides = []
            for part in range(2):
                sides.append(
                    jnp.concatenate(
                        [
                            ao_ref[s, pl.ds(((pair * 2 + h) * 5 + k) * 2 + part, 40, stride=100), :]
                            for h in range(2)
                        ],
                        0,
                    )
                )
            hi, lo = halves(jnp.concatenate(sides, 1))
            at = pl.ds(pl.multiple_of(pair * 80, 16), 80)
            x_hi[k, at, :] = hi
            x_lo[k, at, :] = lo
        return 0

    lax.fori_loop(0, 5, load, 0)
    carry = None
    for k, blocks in enumerate(TILES):
        width = 128 * len(blocks)
        wh, wl = w_hi[k, :, :width], w_lo[k, :, :width]
        xh, xl = x_hi[k], x_lo[k]
        y = dot(xh, wh) + dot(xh, wl) + dot(xl, wh)
        for b, (m, start) in enumerate(blocks):
            value = y[:, 128 * b : 128 * b + 128]
            if start < 0:
                value = value + carry
            if start + 80 > 128:
                carry = value
                continue
            for g in range(10):
                t1[pl.ds(8 * g + m, 40, stride=80), :] = value[40 * g : 40 * g + 40]

    occ = jnp.concatenate([occ_ref[s, 0], occ_ref[s, 1]], 0)
    c_hi, c_lo = halves(occ)
    c_both = jnp.concatenate([c_hi, c_lo], 0)
    sign = jnp.where(lax.broadcasted_iota(jnp.int32, (16, 128), 1) < 64, 1.0, -1.0).astype(F32)

    def second(pair, _):
        rows = t1[pl.ds(pl.multiple_of(pair * 160, 8), 160), :]
        hi, lo = halves(jnp.concatenate([rows[:80], rows[80:]], 1))
        both = dot(c_both, hi)
        u = both[:32] + both[32:] + dot(c_hi, lo)
        for h in range(2):
            ure, uim = u[:16, 128 * h : 128 * h + 128], u[16:, 128 * h : 128 * h + 128]
            put(pair * 2 + h, ure + sign * swap_sides(uim))
        return 0

    lax.fori_loop(0, 20, second, 0, unroll=4)


def select_kernel(
    place, rows, diff, label, occ_ref, vir_ref, occ_e, vir_e, occ_out, vir_out, base_ref, occr_ref
):
    s = pl.program_id(0)
    occ_out[s] = occ_ref[0]
    vir_out[s] = vir_ref[0]

    @pl.when(s == 0)
    def _():
        slot, i = place[0], place[1]
        other = slot + 1 - 2 * (slot % 2)
        col = lax.broadcasted_iota(jnp.int32, (32, 64), 1)
        row = lax.broadcasted_iota(jnp.int32, (32, 64), 0)
        low = lax.broadcasted_iota(jnp.int32, (32, 128), 1) < 64
        lane = lax.broadcasted_iota(jnp.int32, (1, 16), 1)
        eye = lax.broadcasted_iota(jnp.int32, (16, 16), 0) == lax.broadcasted_iota(jnp.int32, (16, 16), 1)
        for b in range(2):
            ki = rows[slot, b]
            ka = diff[ki, label[slot]]
            occ_left = jnp.sum(jnp.where(lane == i, occ_e[pl.ds(ki, 1), :], 0.0), axis=1, keepdims=True)
            line = vir_e[pl.ds(ka, 1), :]
            even = jnp.sum(jnp.where(col == 2 * row, line, 0.0), axis=1, keepdims=True)
            odd = jnp.sum(jnp.where(col == 2 * row + 1, line, 0.0), axis=1, keepdims=True)
            left = occ_left - jnp.where(low, even, odd)
            for t in range(2):
                kj = rows[other, 2 + t]
                kb = diff[kj, label[other]]
                right = vir_e[pl.ds(kb, 1), :]
                base_ref[2 * b + t] = left - jnp.concatenate([right, right], 1)
                if b == 0:
                    occ_right = jnp.sum(jnp.where(eye, occ_e[pl.ds(kj, 1), :], 0.0), axis=1, keepdims=True)
                    occr_ref[t] = jnp.broadcast_to(occ_right, (16, 128))


def select(place, rows, diff, label, occ, vir, occ_e, vir_e):
    def occ_at(s, place, rows, diff, label):
        return (rows[place[0], s], 0, 0, 0)

    def vir_at(s, place, rows, diff, label):
        return (diff[rows[place[0], s], label[place[0]]], 0, 0, 0)

    def whole(*shape):
        return pl.BlockSpec(shape, lambda s, *_: (0,) * len(shape))

    shapes = ((4, 2, 16, 80), (4, 2, 64, 80), (4, 32, 128), (2, 16, 128))
    return pl.pallas_call(
        select_kernel,
        out_shape=tuple(jax.ShapeDtypeStruct(shape, F32) for shape in shapes),
        grid_spec=pltpu.PrefetchScalarGridSpec(
            num_scalar_prefetch=4,
            grid=(4,),
            in_specs=[
                pl.BlockSpec((1, 2, 16, 80), occ_at),
                pl.BlockSpec((1, 2, 64, 80), vir_at),
                whole(27, 16),
                whole(27, 64),
            ],
            out_specs=tuple(whole(*shape) for shape in shapes),
        ),
        compiler_params=pltpu.CompilerParams(vmem_limit_bytes=48 * 2**20),
        name="select",
    )(place, rows, diff, label, occ, vir, occ_e, vir_e)


POS = {0: 0, 1: 1, -1: 2, 2: 3, -2: 4, 3: 5, -3: 6, 4: 7, -4: 7}
STAGES = ((0, 240), (240, 400), (400, 640))
CHUNKS = 4
LINES = 32 // CHUNKS


def pair_kernel(
    ao_hbm, occ_ref, vir_ref, base_ref, occr_ref, out_ref,
    ao_ref, w_hi, w_lo, x_hi, x_lo, t1, lr_ref, rbuf, lbuf, lt_hi, lt_lo, ybuf,
    ao_sem, par_send, par_recv, hop_send, hop_recv, sib_send, sib_recv, l_send, l_recv, own_sem,
):
    pb, aux = lax.axis_index("pb"), lax.axis_index("aux")
    z, c = aux // 2, aux % 2
    partner = pb + 1 - 2 * (pb % 2)
    sibling = aux + 1 - 2 * c

    def at_z(dz, core):
        return lax.rem(z + dz + 8, 8) * 2 + core

    barrier = pltpu.get_barrier_semaphore()
    for far in range(1, 16):
        pl.semaphore_signal(barrier, inc=1, device_id={"aux": lax.rem(aux + far, 16)}, device_id_type=MESH)
    pl.semaphore_signal(barrier, inc=1, device_id={"pb": partner}, device_id_type=MESH)

    blocks = {s: pltpu.make_async_copy(ao_hbm.at[s], ao_ref.at[s], ao_sem.at[s]) for s in (0, 2, 1, 3)}
    for copy in blocks.values():
        copy.start()
    w_hi[...] = jnp.zeros_like(w_hi)
    w_lo[...] = jnp.zeros_like(w_lo)

    def make(s):
        blocks[s].wait()

        def put(p, value):
            lr_ref.reshape(2560, 128)[pl.ds(s * 640 + p, 16, stride=40), :] = value

        orbitals(s, ao_ref, occ_ref, vir_ref, put, w_hi, w_lo, x_hi, x_lo, t1)

    def place(pos, core):
        return pl.ds(pl.multiple_of(pos * 80 + core * 40, 8), 40)

    def chunk(pos, q):
        return rbuf.at[pl.ds(LINES * q, LINES), place(pos, c), :]

    def partner_copy(q):
        return pltpu.make_async_remote_copy(
            lr_ref.at[pl.ds(32 + LINES * q, LINES)], chunk(0, q), par_send.at[q], par_recv.at[q],
            device_id={"pb": partner}, device_id_type=MESH,
        )

    def hop_copy(way, d, q):
        step = 1 - 2 * way
        return pltpu.make_async_remote_copy(
            chunk(POS[-step * (d - 1)], q), chunk(POS[-step * d], q),
            hop_send.at[way, d - 1, q], hop_recv.at[way, d - 1, q],
            device_id={"aux": at_z(step, c)}, device_id_type=MESH,
        )

    def sibling_copy(pos, q):
        return pltpu.make_async_remote_copy(
            chunk(pos, q), chunk(pos, q), sib_send.at[pos, q], sib_recv.at[pos, q],
            device_id={"aux": sibling}, device_id_type=MESH,
        )

    def row_copy(s, dz, cross):
        core = c + cross * (1 - 2 * c)
        to = at_z(dz, core)
        pos = POS[-dz]
        src, dst = lr_ref.at[16 * s + to], lbuf.at[s, place(pos, c), :]
        if dz == 0 and cross == 0:
            return pltpu.make_async_copy(src, dst, own_sem.at[s])
        return pltpu.make_async_remote_copy(
            src, dst, l_send.at[s, pos, cross], l_recv.at[s, pos, cross],
            device_id={"aux": to}, device_id_type=MESH,
        )

    rows = {
        (s, dz, cross): row_copy(s, dz, cross)
        for s in range(2) for dz in (4, 3, -3, 2, -2, 1, -1, 0) for cross in range(2)
    }
    partners = [partner_copy(q) for q in range(CHUNKS)]
    sent = []

    def send(copy):
        copy.start()
        sent.append(copy)

    def send_rows(s):
        for (block, _, _), copy in rows.items():
            if block == s:
                copy.start()

    def send_partner(t):
        for q in range(CHUNKS):
            if q * LINES // 16 == t:
                partners[q].start()

    def has_hop(way, d, q):
        return d < 4 or q * LINES // 16 == way

    def relay(d, q):
        for way in range(2):
            if not has_hop(way, d, q):
                continue
            hop_copy(way, d, q).wait_recv()
            if d < 4 and has_hop(way, d + 1, q):
                send(hop_copy(way, d + 1, q))
            send(sibling_copy(POS[-d if way == 0 else d], q))

    def left_sides():
        for (s, dz, cross), copy in rows.items():
            if dz == 0 and cross == 0:
                copy.wait()
            else:
                copy.wait_recv()
        for n, (first, last) in enumerate(STAGES):
            for s in range(2):
                part = lbuf[s, first:last, :]
                part = jnp.concatenate([part, jnp.zeros((256 - (last - first), 128), F32)], 0)
                hi, lo = halves(part.T)
                lt_hi[n, 128 * s : 128 * s + 128, :] = hi
                lt_lo[n, 128 * s : 128 * s + 128, :] = lo

    low = lax.broadcasted_iota(jnp.int32, (32, 128), 1) < 64

    def finish(n):
        t, j = n // 16, n % 16
        for s in range(2):
            def half(part, odd):
                return ybuf[n, pl.ds(128 * s + 64 * part + odd, 32, stride=2), :]

            re_e, re_d, im_e, im_d = half(0, 0), half(0, 1), half(1, 0), half(1, 1)
            inverse = 1.0 / (base_ref[2 * s + t] + occr_ref[t, pl.ds(j, 1), :])
            real = jnp.where(low, re_e, swap_sides(re_d)) - jnp.where(low, swap_sides(im_e), im_d)
            imag = jnp.where(low, swap_sides(re_e), re_d) + jnp.where(low, im_e, swap_sides(im_d))
            for part, value in enumerate((real, imag)):
                first = ((part * 2 + s) * 2 + t) * 512 + (j // 8) * 256 + j % 8
                out_ref[pl.ds(first, 32, stride=8), :] = value * inverse

    def multiply(stage, q):
        first, last = STAGES[stage]
        width = last - first

        def body(pair, _):
            n = LINES * q + pair * 2
            r = jnp.concatenate([rbuf[n + h, first:last, :] for h in range(2)], 1)
            hi, lo = halves(r)
            lh, ll = lt_hi[stage, :, :width], lt_lo[stage, :, :width]
            y = dot(lh, hi) + dot(ll, hi) + dot(lh, lo)
            for h in range(2):
                value = y[:, 128 * h : 128 * h + 128]
                if stage > 0:
                    value = value + ybuf[n + h]
                ybuf[n + h] = value
                if stage == 2:
                    finish(n + h)
            return 0

        lax.fori_loop(0, LINES // 2, body, 0)

    def from_sibling(q, *positions):
        for pos in positions:
            sibling_copy(pos, q).wait_recv()

    def open_ring(q):
        partners[q].wait_recv()
        for way in range(2):
            send(hop_copy(way, 1, q))
        send(sibling_copy(0, q))

    make(0)
    pl.semaphore_wait(barrier, 16)
    send_rows(0)
    make(2)
    send_partner(0)
    make(1)
    send_rows(1)
    make(3)
    send_partner(1)
    for q in range(CHUNKS):
        open_ring(q)
    for q in range(CHUNKS):
        relay(1, q)
    left_sides()
    for q in range(CHUNKS):
        relay(2, q)
        from_sibling(q, 0, 1, 2)
        multiply(0, q)
    for q in range(CHUNKS):
        relay(3, q)
        from_sibling(q, 3, 4)
        multiply(1, q)
    for half in range(CHUNKS // 2):
        for q in (half, half + CHUNKS // 2):
            relay(4, q)
        for q in (half, half + CHUNKS // 2):
            from_sibling(q, 5, 6, 7)
            multiply(2, q)
    for copy in partners + sent:
        copy.wait_send()
    for (s, dz, cross), copy in rows.items():
        if dz != 0 or cross != 0:
            copy.wait_send()


def pair_sums(ao, occ, vir, base, occr):
    vmem = pl.BlockSpec(memory_space=pltpu.VMEM)
    dma = pltpu.SemaphoreType.DMA
    return pl.pallas_call(
        pair_kernel,
        out_shape=jax.ShapeDtypeStruct((4096, 128), F32),
        in_specs=[pl.BlockSpec(memory_space=pl.ANY), vmem, vmem, vmem, vmem],
        out_specs=vmem,
        scratch_shapes=[
            pltpu.VMEM((4, 4000, 128), F32),
            pltpu.VMEM((5, 256, 384), BF16),
            pltpu.VMEM((5, 256, 384), BF16),
            pltpu.VMEM((5, 400, 256), BF16),
            pltpu.VMEM((5, 400, 256), BF16),
            pltpu.VMEM((3200, 128), F32),
            pltpu.VMEM((64, 40, 128), F32),
            pltpu.VMEM((32, 640, 128), F32),
            pltpu.VMEM((2, 640, 128), F32),
            pltpu.VMEM((3, 256, 256), BF16),
            pltpu.VMEM((3, 256, 256), BF16),
            pltpu.VMEM((32, 256, 128), F32),
            dma((4,)),
            dma((CHUNKS,)), dma((CHUNKS,)),
            dma((2, 4, CHUNKS)), dma((2, 4, CHUNKS)),
            dma((8, CHUNKS)), dma((8, CHUNKS)),
            dma((2, 8, 2)), dma((2, 8, 2)),
            dma((2,)),
        ],
        compiler_params=pltpu.CompilerParams(
            collective_id=0, has_side_effects=True, vmem_limit_bytes=48 * 2**20
        ),
        cost_estimate=pl.CostEstimate(flops=6 * 10**9, bytes_accessed=12 * 10**6, transcendentals=0),
        name="pair_sums",
    )(ao, occ, vir, base, occr)


def per_device(
    ao_blocks, occ_coef, vir_coef, occ_energy, vir_energy, kpoint_diff, transfer_label, chosen_rows
):
    place = jnp.stack([lax.axis_index("pb"), lax.axis_index("aux")]).astype(jnp.int32)
    ao = with_layout_constraint(
        ao_blocks.reshape(4, 40, 2, 50, 128), Layout(major_to_minor=(0, 1, 3, 2, 4))
    )
    ao = ao.transpose(0, 1, 3, 2, 4).reshape(4, 4000, 128)
    occ, vir, base, occr = select(
        place, chosen_rows, kpoint_diff, transfer_label,
        occ_coef.swapaxes(2, 3), vir_coef.swapaxes(2, 3), occ_energy, vir_energy,
    )
    out = pair_sums(ao, occ, vir, base, occr)
    out = out.reshape(2, 2, 2, 2, 32, 8, 128).transpose(0, 1, 2, 3, 5, 4, 6)
    return out.reshape(1, 2, 2, 2, 1, 16, 4096)


def solution(mesh):
    in_specs = (P("pb", None, "aux", None, None), P(), P(), P(), P(), P(), P(), P())
    out_specs = P("pb", None, None, None, "aux", None, None)
    return jax.shard_map(
        per_device, mesh=mesh, in_specs=in_specs, out_specs=out_specs, check_vma=False
    )
```

time: 110 us -> 91.7 us (0.83)
  Pallas kernels: 98.6 us -> 83.9 us
  local copies, waits for them, and re-layouts: 10.8 us -> 7.44 us
    pallas_call x1, Pallas kernels: 14.2 us -> 1.19 us  [select(): pl.pallas_call(select_kernel, out_shape=tuple((jax.ShapeDtypeStruct(shape...]
    unnamed x15 -> x13, local copies, waits for them, and re-layouts: 10.8 us -> 7.44 us
    pallas_call x1, Pallas kernels: 84.4 us -> 82.7 us  [pair_sums(): pl.pallas_call(pair_kernel, out_shape=jax.ShapeDtypeStruct((4096, 128), F...]
where the time goes in v3:
time: 91.7 us; the launch traced here: 91.4 us
  Pallas kernels  83.9 us (91%)
  local copies, waits for them, and re-layouts  7.44 us (8%)
    pallas_call x1, Pallas kernels, pair_sums(): pl.pallas_call(pair_kernel, out_shape=jax.ShapeDtypeStruct((4096, 128), F...  82.7 us
    unnamed x13, local copies, waits for them, and re-layouts  7.44 us

profile of v3, /device:TPU:1, one launch (start us, length us, event | category | flops | bytes accessed | tf_op | source)
XLA Modules:
  0.0 91.4 jit_solution(17280692470360624460)
XLA Ops:
  0.0 0.1 pad_add_fusion.place
  0.1 0.8 copy.9.rows
  0.8 0.8 copy.10.occ_e
  1.6 0.0 copy-start
  1.6 1.5 %copy-done = f32[27,2,80,64]{2,3,1,0:T(8,128)S(1)} copy-done((f32[27,2,80,64]{2,3,1,0:T(8,128)S(1)}, f32[27,2,80,64]{2,3,1,0:T(8,128)}, u32[]{:S(2)}) %copy-start) | copy-done | bytes 1105944
  3.1 0.0 copy-start.1
  3.1 1.0 %copy-done.1 = f32[27,2,80,16]{2,3,1,0:T(8,128)S(1)} copy-done((f32[27,2,80,16]{2,3,1,0:T(8,128)S(1)}, f32[27,2,80,16]{2,3,1,0:T(8,128)}, u32[]{:S(2)}) %copy-start.1) | copy-done | bytes 276504
  4.1 0.0 copy-start.2
  4.1 0.7 copy-done.2
  4.8 0.0 copy-start.3
  4.8 0.7 copy-done.3
  5.5 0.0 copy-start.4
  5.5 0.7 copy-done.4
  6.2 1.2 %select.1 = (f32[4,2,16,80]{3,2,1,0:T(8,128)S(1)}, f32[4,2,64,80]{3,2,1,0:T(8,128)S(1)}, f32[4,32,128]{2,1,0:T(8,128)S(1)}, f32[2,16,128]{2,1,0:T(8,128)S(1)}) custom-call(s32[2]{0:T(128)S(1)} %pad_add_fusion.place, s32[16,4]{1,0:T(8,128)S(1)} %copy.9.rows, s32[27,27]{1,0:T(8,128)S(1)} %copy-done.2, s32[16]{0:T(128)S(1)} %copy-done.4, ...), custom_call_target="tpu_custom_call" | custom-call | tf_op jit(solution)/shard_map/select/pallas_call | solution.py:150
  7.4 82.7 %pair_sums.1 = f32[4096,128]{1,0:T(8,128)S(1)} custom-call(f32[4,4000,128]{2,1,0:T(8,128)} %bitcast.17, f32[4,2,16,80]{3,2,1,0:T(8,128)S(1)} %get-tuple-element.9.occ_ref, f32[4,2,64,80]{3,2,1,0:T(8,128)S(1)} %get-tuple-element.10.vir_ref, f32[4,32,128]{2,1,0:T(8,128)S(1)} %get-tuple-element.11.base_ref, f32[2,16,128]{2,1,0:T(8,128)S(1)} %get-tuple-element.12.occr_ref), custom_call_target="tpu_custom_call" | custom-call | flops 6000000000 | bytes 12000000 | tf_op jit(solution)/shard_map/pair_sums/pallas_call | solution.py:377
  90.1 1.3 %copy.12 = f32[1,2,2,2,1,16,4096]{6,5,4,3,2,1,0:T(8,128)} copy(f32[1,2,2,2,1,16,4096]{6,5,4,3,2,1,0:T(8,128)S(1)} %bitcast.14) | data formatting | bytes 4194304
Async XLA Ops:
  1.6 1.5 %copy-start = (f32[27,2,80,64]{2,3,1,0:T(8,128)S(1)}, f32[27,2,80,64]{2,3,1,0:T(8,128)}, u32[]{:S(2)}) copy-start(f32[27,2,80,64]{2,3,1,0:T(8,128)} %param.10) | copy-start | bytes 3317764
  3.1 1.0 %copy-start.1 = (f32[27,2,80,16]{2,3,1,0:T(8,128)S(1)}, f32[27,2,80,16]{2,3,1,0:T(8,128)}, u32[]{:S(2)}) copy-start(f32[27,2,80,16]{2,3,1,0:T(8,128)} %param.9) | copy-start | bytes 829444
  4.1 0.7 copy-start.2
  4.8 0.7 copy-start.3
  5.5 0.7 copy-start.4

commit v4 on v3

--- a/solution.py
+++ b/solution.py
@@ -1,5 +1,3 @@
-import functools
-
 import jax
 import jax.numpy as jnp
 from jax import lax
@@ -31,8 +29,7 @@
     return pltpu.roll(x, 64, 1)
 
 
-def fill_weights(vir_ref, s, w_hi, w_lo):
-    vre, vim = vir_ref[s, 0], vir_ref[s, 1]
+def fill_weights(vre, vim, w_hi, w_lo):
     pad = jnp.zeros((128, 48), F32)
     for part, top, bottom in ((0, vre, vim), (1, -vim, vre)):
         stacked = jnp.concatenate([jnp.concatenate([top, bottom], 0), pad], 1)
@@ -45,8 +42,8 @@
                 w_lo[to] = lo[first - start : last - start]
 
 
-def orbitals(s, ao_ref, occ_ref, vir_ref, put, w_hi, w_lo, x_hi, x_lo, t1):
-    fill_weights(vir_ref, s, w_hi, w_lo)
+def orbitals(s, ao_ref, occ, vre, vim, put, w_hi, w_lo, x_hi, x_lo, t1):
+    fill_weights(vre, vim, w_hi, w_lo)
 
     def load(pair, _):
         for k in range(5):
@@ -84,7 +81,6 @@
             for g in range(10):
                 t1[pl.ds(8 * g + m, 40, stride=80), :] = value[40 * g : 40 * g + 40]
 
-    occ = jnp.concatenate([occ_ref[s, 0], occ_ref[s, 1]], 0)
     c_hi, c_lo = halves(occ)
     c_both = jnp.concatenate([c_hi, c_lo], 0)
     sign = jnp.where(lax.broadcasted_iota(jnp.int32, (16, 128), 1) < 64, 1.0, -1.0).astype(F32)
@@ -102,70 +98,6 @@
     lax.fori_loop(0, 20, second, 0, unroll=4)
 
 
-def select_kernel(
-    place, rows, diff, label, occ_ref, vir_ref, occ_e, vir_e, occ_out, vir_out, base_ref, occr_ref
-):
-    s = pl.program_id(0)
-    occ_out[s] = occ_ref[0]
-    vir_out[s] = vir_ref[0]
-
-    @pl.when(s == 0)
-    def _():
-        slot, i = place[0], place[1]
-        other = slot + 1 - 2 * (slot % 2)
-        col = lax.broadcasted_iota(jnp.int32, (32, 64), 1)
-        row = lax.broadcasted_iota(jnp.int32, (32, 64), 0)
-        low = lax.broadcasted_iota(jnp.int32, (32, 128), 1) < 64
-        lane = lax.broadcasted_iota(jnp.int32, (1, 16), 1)
-        eye = lax.broadcasted_iota(jnp.int32, (16, 16), 0) == lax.broadcasted_iota(jnp.int32, (16, 16), 1)
-        for b in range(2):
-            ki = rows[slot, b]
-            ka = diff[ki, label[slot]]
-            occ_left = jnp.sum(jnp.where(lane == i, occ_e[pl.ds(ki, 1), :], 0.0), axis=1, keepdims=True)
-            line = vir_e[pl.ds(ka, 1), :]
-            even = jnp.sum(jnp.where(col == 2 * row, line, 0.0), axis=1, keepdims=True)
-            odd = jnp.sum(jnp.where(col == 2 * row + 1, line, 0.0), axis=1, keepdims=True)
-            left = occ_left - jnp.where(low, even, odd)
-            for t in range(2):
-                kj = rows[other, 2 + t]
-                kb = diff[kj, label[other]]
-                right = vir_e[pl.ds(kb, 1), :]
-                base_ref[2 * b + t] = left - jnp.concatenate([right, right], 1)
-                if b == 0:
-                    occ_right = jnp.sum(jnp.where(eye, occ_e[pl.ds(kj, 1), :], 0.0), axis=1, keepdims=True)
-                    occr_ref[t] = jnp.broadcast_to(occ_right, (16, 128))
-
-
-def select(place, rows, diff, label, occ, vir, occ_e, vir_e):
-    def occ_at(s, place, rows, diff, label):
-        return (rows[place[0], s], 0, 0, 0)
-
-    def vir_at(s, place, rows, diff, label):
-        return (diff[rows[place[0], s], label[place[0]]], 0, 0, 0)
-
-    def whole(*shape):
-        return pl.BlockSpec(shape, lambda s, *_: (0,) * len(shape))
-
-    shapes = ((4, 2, 16, 80), (4, 2, 64, 80), (4, 32, 128), (2, 16, 128))
-    return pl.pallas_call(
-        select_kernel,
-        out_shape=tuple(jax.ShapeDtypeStruct(shape, F32) for shape in shapes),
-        grid_spec=pltpu.PrefetchScalarGridSpec(
-            num_scalar_prefetch=4,
-            grid=(4,),
-            in_specs=[
-                pl.BlockSpec((1, 2, 16, 80), occ_at),
-                pl.BlockSpec((1, 2, 64, 80), vir_at),
-                whole(27, 16),
-                whole(27, 64),
-            ],
-            out_specs=tuple(whole(*shape) for shape in shapes),
-        ),
-        compiler_params=pltpu.CompilerParams(vmem_limit_bytes=48 * 2**20),
-        name="select",
-    )(place, rows, diff, label, occ, vir, occ_e, vir_e)
-
-
 POS = {0: 0, 1: 1, -1: 2, 2: 3, -2: 4, 3: 5, -3: 6, 4: 7, -4: 7}
 STAGES = ((0, 240), (240, 400), (400, 640))
 CHUNKS = 4
@@ -173,9 +105,9 @@
 
 
 def pair_kernel(
-    ao_hbm, occ_ref, vir_ref, base_ref, occr_ref, out_ref,
-    ao_ref, w_hi, w_lo, x_hi, x_lo, t1, lr_ref, rbuf, lbuf, lt_hi, lt_lo, ybuf,
-    ao_sem, par_send, par_recv, hop_send, hop_recv, sib_send, sib_recv, l_send, l_recv, own_sem,
+    ao_hbm, occ_hbm, vir_hbm, occ_e_hbm, vir_e_hbm, diff_hbm, label_hbm, rows_hbm, out_ref,
+    occ_ref, vir_ref, occ_e, vir_e, diff, label, chosen, base_ref, occr_ref, ao_ref, w_hi, w_lo, x_hi, x_lo, t1, lr_ref, rbuf, lbuf, lt_hi, lt_lo, ybuf,
+    in_sem, ao_sem, par_send, par_recv, hop_send, hop_recv, sib_send, sib_recv, l_send, l_recv, own_sem,
 ):
     pb, aux = lax.axis_index("pb"), lax.axis_index("aux")
     z, c = aux // 2, aux % 2
@@ -190,19 +122,58 @@
         pl.semaphore_signal(barrier, inc=1, device_id={"aux": lax.rem(aux + far, 16)}, device_id_type=MESH)
     pl.semaphore_signal(barrier, inc=1, device_id={"pb": partner}, device_id_type=MESH)
 
+    inputs = [
+        pltpu.make_async_copy(src, dst, in_sem.at[n])
+        for n, (src, dst) in enumerate(
+            (
+                (rows_hbm, chosen), (diff_hbm, diff), (label_hbm, label), (vir_hbm, vir_ref),
+                (occ_hbm, occ_ref), (occ_e_hbm, occ_e), (vir_e_hbm, vir_e),
+            )
+        )
+    ]
+    for copy in inputs:
+        copy.start()
     blocks = {s: pltpu.make_async_copy(ao_hbm.at[s], ao_ref.at[s], ao_sem.at[s]) for s in (0, 2, 1, 3)}
     for copy in blocks.values():
         copy.start()
     w_hi[...] = jnp.zeros_like(w_hi)
     w_lo[...] = jnp.zeros_like(w_lo)
 
+    for copy in inputs:
+        copy.wait()
+
+    def energies():
+        col = lax.broadcasted_iota(jnp.int32, (32, 64), 1)
+        row = lax.broadcasted_iota(jnp.int32, (32, 64), 0)
+        first_lanes = lax.broadcasted_iota(jnp.int32, (32, 128), 1) < 64
+
+        def pick(values, k):
+            lane = lax.broadcasted_iota(jnp.int32, values.shape, 1)
+            return jnp.sum(jnp.where(lane == k, values, 0.0), axis=1, keepdims=True)
+
+        for b in range(2):
+            ki = chosen[b, pb]
+            line = vir_e[pl.ds(diff[ki, label[pb]], 1), :]
+            even = jnp.sum(jnp.where(col == 2 * row, line, 0.0), axis=1, keepdims=True)
+            odd = jnp.sum(jnp.where(col == 2 * row + 1, line, 0.0), axis=1, keepdims=True)
+            left = pick(occ_e[pl.ds(aux, 1), :], ki) - jnp.where(first_lanes, even, odd)
+            for t in range(2):
+                kj = chosen[2 + t, partner]
+                right = vir_e[pl.ds(diff[kj, label[partner]], 1), :]
+                base_ref[2 * b + t] = left - jnp.concatenate([right, right], 1)
+                if b == 0:
+                    occr_ref[t] = jnp.broadcast_to(pick(occ_e[...], kj), (16, 128))
+
     def make(s):
         blocks[s].wait()
+        k = chosen[s, pb]
+        ka = diff[k, label[pb]]
+        occ = jnp.concatenate([occ_ref[k, 0], occ_ref[k, 1]], 0)
 
         def put(p, value):
             lr_ref.reshape(2560, 128)[pl.ds(s * 640 + p, 16, stride=40), :] = value
 
-        orbitals(s, ao_ref, occ_ref, vir_ref, put, w_hi, w_lo, x_hi, x_lo, t1)
+        orbitals(s, ao_ref, occ, vir_ref[ka, 0], vir_ref[ka, 1], put, w_hi, w_lo, x_hi, x_lo, t1)
 
     def place(pos, core):
         return pl.ds(pl.multiple_of(pos * 80 + core * 40, 8), 40)
@@ -341,6 +312,7 @@
     send_rows(0)
     make(2)
     send_partner(0)
+    energies()
     make(1)
     send_rows(1)
     make(3)
@@ -371,15 +343,23 @@
             copy.wait_send()
 
 
-def pair_sums(ao, occ, vir, base, occr):
-    vmem = pl.BlockSpec(memory_space=pltpu.VMEM)
+def pair_sums(*operands):
     dma = pltpu.SemaphoreType.DMA
     return pl.pallas_call(
         pair_kernel,
         out_shape=jax.ShapeDtypeStruct((4096, 128), F32),
-        in_specs=[pl.BlockSpec(memory_space=pl.ANY), vmem, vmem, vmem, vmem],
-        out_specs=vmem,
+        in_specs=[pl.BlockSpec(memory_space=pltpu.HBM)] * 8,
+        out_specs=pl.BlockSpec(memory_space=pltpu.VMEM),
         scratch_shapes=[
+            pltpu.VMEM((27, 2, 16, 80), F32),
+            pltpu.VMEM((27, 2, 64, 80), F32),
+            pltpu.VMEM((16, 27), F32),
+            pltpu.VMEM((27, 64), F32),
+            pltpu.SMEM((27, 27), jnp.int32),
+            pltpu.SMEM((16,), jnp.int32),
+            pltpu.SMEM((4, 16), jnp.int32),
+            pltpu.VMEM((4, 32, 128), F32),
+            pltpu.VMEM((2, 16, 128), F32),
             pltpu.VMEM((4, 4000, 128), F32),
             pltpu.VMEM((5, 256, 384), BF16),
             pltpu.VMEM((5, 256, 384), BF16),
@@ -392,6 +372,7 @@
             pltpu.VMEM((3, 256, 256), BF16),
             pltpu.VMEM((3, 256, 256), BF16),
             pltpu.VMEM((32, 256, 128), F32),
+            dma((7,)),
             dma((4,)),
             dma((CHUNKS,)), dma((CHUNKS,)),
             dma((2, 4, CHUNKS)), dma((2, 4, CHUNKS)),
@@ -400,26 +381,24 @@
             dma((2,)),
         ],
         compiler_params=pltpu.CompilerParams(
-            collective_id=0, has_side_effects=True, vmem_limit_bytes=48 * 2**20
+            collective_id=0, has_side_effects=True, vmem_limit_bytes=56 * 2**20
         ),
         cost_estimate=pl.CostEstimate(flops=6 * 10**9, bytes_accessed=12 * 10**6, transcendentals=0),
         name="pair_sums",
-    )(ao, occ, vir, base, occr)
+    )(*operands)
 
 
 def per_device(
     ao_blocks, occ_coef, vir_coef, occ_energy, vir_energy, kpoint_diff, transfer_label, chosen_rows
 ):
-    place = jnp.stack([lax.axis_index("pb"), lax.axis_index("aux")]).astype(jnp.int32)
     ao = with_layout_constraint(
         ao_blocks.reshape(4, 40, 2, 50, 128), Layout(major_to_minor=(0, 1, 3, 2, 4))
     )
     ao = ao.transpose(0, 1, 3, 2, 4).reshape(4, 4000, 128)
-    occ, vir, base, occr = select(
-        place, chosen_rows, kpoint_diff, transfer_label,
-        occ_coef.swapaxes(2, 3), vir_coef.swapaxes(2, 3), occ_energy, vir_energy,
+    out = pair_sums(
+        ao, occ_coef.swapaxes(2, 3), vir_coef.swapaxes(2, 3), occ_energy.T, vir_energy,
+        kpoint_diff, transfer_label, chosen_rows.T,
     )
-    out = pair_sums(ao, occ, vir, base, occr)
     out = out.reshape(2, 2, 2, 2, 32, 8, 128).transpose(0, 1, 2, 3, 5, 4, 6)
     return out.reshape(1, 2, 2, 2, 1, 16, 4096)
 

time: 91.7 us -> 88.6 us (0.966)
  local copies, waits for them, and re-layouts: 7.44 us -> 3.11 us
  Pallas kernels: 83.9 us -> 85.4 us
    unnamed x13 -> x1, local copies, waits for them, and re-layouts: 7.44 us -> 3.11 us
    pallas_call x1, Pallas kernels: 82.7 us -> 85.4 us  [pair_sums(): pl.pallas_call(pair_kernel, out_shape=jax.ShapeDtypeStruct((4096, 128), F...]
    pallas_call x1 -> x0, Pallas kernels: 1.19 us -> none  [select(): pl.pallas_call(select_kernel, out_shape=tuple((jax.ShapeDtypeStruct(shape...]
where the time goes in v4:
time: 88.6 us; the launch traced here: 88.5 us
  Pallas kernels  85.4 us (96%)
  local copies, waits for them, and re-layouts  3.11 us (4%)
    pallas_call x1, Pallas kernels, pair_sums(): pl.pallas_call(pair_kernel, out_shape=jax.ShapeDtypeStruct((4096, 128), F...  85.4 us
    unnamed x1, local copies, waits for them, and re-layouts  3.11 us

profile of v4, /device:TPU:1, one launch (start us, length us, event | category | flops | bytes accessed | tf_op | source)
XLA Modules:
  0.0 88.5 jit_solution(10759230353619660028)
XLA Ops:
  0.0 85.4 %pair_sums.1 = f32[4096,128]{1,0:T(8,128)} custom-call(f32[4,4000,128]{2,1,0:T(8,128)} %bitcast.15, f32[27,2,16,80]{3,2,1,0:T(8,128)} %bitcast.17, f32[27,2,64,80]{3,2,1,0:T(8,128)} %bitcast.16, f32[16,27]{1,0:T(8,128)} %bitcast.18, f32[27,64]{1,0:T(8,128)} %vir_e_hbm.1, s32[27,27]{1,0:T(8,128)} %diff_hbm.1, s32[16]{0:T(128)} %label_hbm.1, s32[4,16]{1,0:T(4,128)} %bitcast.19), custom_call_target="tpu_custom_call" | custom-call | flops 6000000000 | bytes 12000000 | tf_op jit(solution)/shard_map/pair_sums/pallas_call | solution.py:348
  85.4 3.1 %copy.10 = f32[1,2,2,2,1,16,4096]{6,5,4,3,2,1,0:T(8,128)} copy(f32[1,2,2,2,1,16,4096]{6,5,4,3,2,1,0:T(8,128)} %bitcast.14) | data formatting | bytes 4194304

commit v5 on v4

--- a/solution.py
+++ b/solution.py
@@ -64,7 +64,7 @@
             x_lo[k, at, :] = lo
         return 0
 
-    lax.fori_loop(0, 5, load, 0)
+    lax.fori_loop(0, 5, load, 0, unroll=5)
     carry = None
     for k, blocks in enumerate(TILES):
         width = 128 * len(blocks)
@@ -95,7 +95,7 @@
             put(pair * 2 + h, ure + sign * swap_sides(uim))
         return 0
 
-    lax.fori_loop(0, 20, second, 0, unroll=4)
+    lax.fori_loop(0, 20, second, 0, unroll=10)
 
 
 POS = {0: 0, 1: 1, -1: 2, 2: 3, -2: 4, 3: 5, -3: 6, 4: 7, -4: 7}
@@ -295,7 +295,7 @@
                     finish(n + h)
             return 0
 
-        lax.fori_loop(0, LINES // 2, body, 0)
+        lax.fori_loop(0, LINES // 2, body, 0, unroll=4)
 
     def from_sibling(q, *positions):
         for pos in positions:

time: 88.6 us -> 85.9 us (0.970)
  Pallas kernels: 85.4 us -> 82.7 us
    pallas_call x1, Pallas kernels: 85.4 us -> 82.7 us  [pair_sums(): pl.pallas_call(pair_kernel, out_shape=jax.ShapeDtypeStruct((4096, 128), F...]
where the time goes in v5:
time: 85.9 us; the launch traced here: 85.8 us
  Pallas kernels  82.7 us (96%)
  local copies, waits for them, and re-layouts  3.11 us (4%)
    pallas_call x1, Pallas kernels, pair_sums(): pl.pallas_call(pair_kernel, out_shape=jax.ShapeDtypeStruct((4096, 128), F...  82.7 us
    unnamed x1, local copies, waits for them, and re-layouts  3.11 us

profile of v5, /device:TPU:1, one launch (start us, length us, event | category | flops | bytes accessed | tf_op | source)
XLA Modules:
  0.0 85.8 jit_solution(10779927453195530793)
XLA Ops:
  0.0 82.7 %pair_sums.1 = f32[4096,128]{1,0:T(8,128)} custom-call(f32[4,4000,128]{2,1,0:T(8,128)} %bitcast.15, f32[27,2,16,80]{3,2,1,0:T(8,128)} %bitcast.17, f32[27,2,64,80]{3,2,1,0:T(8,128)} %bitcast.16, f32[16,27]{1,0:T(8,128)} %bitcast.18, f32[27,64]{1,0:T(8,128)} %vir_e_hbm.1, s32[27,27]{1,0:T(8,128)} %diff_hbm.1, s32[16]{0:T(128)} %label_hbm.1, s32[4,16]{1,0:T(4,128)} %bitcast.19), custom_call_target="tpu_custom_call" | custom-call | flops 6000000000 | bytes 12000000 | tf_op jit(solution)/shard_map/pair_sums/pallas_call | solution.py:348
  82.7 3.1 %copy.10 = f32[1,2,2,2,1,16,4096]{6,5,4,3,2,1,0:T(8,128)} copy(f32[1,2,2,2,1,16,4096]{6,5,4,3,2,1,0:T(8,128)} %bitcast.14) | data formatting | bytes 4194304
